TPU v7x, 32 devices: a whole 2x2x4 slice. The times are simulated.
32 devices in a mesh: rep: 4 (over y, x), fsdp: 8 (over z, core).
Axes of the slice: x: 2, y: 2, z: 4, core: 2. Of those that a mesh axis runs over, the one named last changes fastest.
Arguments:
- hidden_acts: bfloat16 [4, 4096, 256], P('rep', 'fsdp'), may hold values from -6 to 6
- out_grads: bfloat16 [4, 4096, 8192], P('rep', 'fsdp'), may hold values from -0.25 to 0.25
- anchor: float32 [256, 8192], P('fsdp'), may hold values from -6 to 6
- drift: float32 [4, 256, 8192], P('rep', 'fsdp'), may hold values from -120 to 120, as said below
- adam_first: float32 [4, 256, 8192], P('rep', 'fsdp'), may hold values from -6 to 6
- adam_second: float32 [4, 256, 8192], P('rep', 'fsdp'), may hold values from 0.3 to 3
- outer_momentum: float32 [256, 8192], P('fsdp'), may hold values from -6 to 6
Outputs:
- new_first: float32 [4, 256, 8192], P('rep', 'fsdp')
- new_second: float32 [4, 256, 8192], P('rep', 'fsdp')
- new_momentum: float32 [256, 8192], P('fsdp')
- new_anchor: float32 [256, 8192], P('fsdp')
Inputs may be any that keep to these rules, and one draw needn't show every extreme that they name: drift entries are finite reals.
All inputs are finite; a program needn't handle non-finite values.
Results may differ from a plain program's by a relative error of at most 0.0003.
Values sent between devices are 32-bit elements; how exact they have to be, the bound alone decides.
A program may use at most 128 MiB of HBM per device.

v0:
```python
import math

import jax
import jax.numpy as jnp
from jax import lax
from jax.sharding import PartitionSpec as P

D = 8192
INNER_STEP = 100


beta_first = 0.9
beta_second = 0.95
inner_rate = 0.5
decay_weight = 0.1
outer_rate = 0.7
momentum_coef = 0.9


def outer_update(average, squares, ceiling, momentum_old, anchor_old):
    factor = ceiling / jnp.maximum(jnp.sqrt(squares), ceiling)
    momentum = momentum_coef * momentum_old + factor * average
    updated = anchor_old - outer_rate * (factor * average + momentum_coef * momentum)
    return (momentum, updated)


def per_device(hidden_acts, out_grads, anchor, drift, adam_first, adam_second, outer_momentum):
    activations = hidden_acts[0]
    cotangent = out_grads[0]
    rows_dev = anchor.shape[0]
    gradient = lax.psum_scatter(
        lax.dot_general(
            activations, cotangent, (((0,), (0,)), ((), ())), preferred_element_type=jnp.float32
        ),
        "fsdp",
        scatter_dimension=0,
        tiled=True,
    )
    correction_one = 1.0 - beta_first**INNER_STEP
    correction_two = 1.0 - beta_second**INNER_STEP
    own_drift = drift[0]
    moment_one = beta_first * adam_first[0] + (1.0 - beta_first) * gradient
    moment_two = beta_second * adam_second[0] + (1.0 - beta_second) * gradient * gradient
    update = moment_one / correction_one / (
        jnp.sqrt(moment_two / correction_two) + 1e-08
    ) + decay_weight * (anchor + own_drift)
    pseudo = inner_rate * update - own_drift
    replicas = lax.axis_size("rep")
    ceiling = 0.3 * math.sqrt(rows_dev * lax.axis_size("fsdp") * D)
    average = lax.psum(pseudo, "rep") / replicas
    squares = lax.psum(jnp.sum(average * average), "fsdp")
    momentum, updated = outer_update(average, squares, ceiling, outer_momentum, anchor)
    return (moment_one[None], moment_two[None], momentum, updated)


def solution(mesh):
    return jax.shard_map(
        per_device,
        mesh=mesh,
        in_specs=(
            P("rep", "fsdp", None),
            P("rep", "fsdp", None),
            P("fsdp", None),
            P("rep", "fsdp", None),
            P("rep", "fsdp", None),
            P("rep", "fsdp", None),
            P("fsdp", None),
        ),
        out_specs=(
            P("rep", "fsdp", None),
            P("rep", "fsdp", None),
            P("fsdp", None),
            P("fsdp", None),
        ),
        check_vma=False,
    )
```

profile of v0, /device:TPU:0, one launch (start us, length us, event | category | flops | bytes accessed | tf_op | source)
XLA Modules:
  0.0 194.2 jit_solution(12159944976548934790)
XLA Ops:
  7.2 0.0 copy-start
  7.2 0.0 reduce-scatter.2.cloned.1.call-start
  7.2 0.9 copy-done
  8.1 9.0 %fusion = f32[256,8192]{1,0:T(8,128)} fusion(bf16[1,512,8192]{2,1,0:T(8,128)(2,1)} %param.8, bf16[1,512,256]{2,1,0:T(8,128)(2,1)S(1)} %copy-done), kind=kOutput, calls=%fused_computation | convolution fusion | flops 2147483648 | bytes 17039360 | tf_op jit(solution)/shard_map/dot_general | solution.py:32
  17.1 0.0 copy-start.1
  17.1 0.0 copy-start.3
  17.1 0.0 copy-start.2
  17.1 0.0 reduce-scatter.2.cloned.1.call-update
  17.1 0.0 all-reduce.2.cloned.1.call-start
  17.2 92.4 %reduce-scatter.2.cloned.1.call-done = f32[32,8192]{1,0:T(8,128)} async-done(((f32[256,8192]{1,0:T(8,128)}), f32[32,8192]{1,0:T(8,128)}) %reduce-scatter.2.cloned.1.call-update) | async-done | bytes 1048592 | tf_op jit(solution)/shard_map/reduce_scatter | solution.py:31
  109.6 0.0 copy-done.1
  109.6 0.0 copy-done.3
  109.6 4.0 %bitcast_subtract_fusion = (f32[32,8192]{1,0:T(8,128)}, f32[1,32,8192]{2,1,0:T(8,128)}, f32[1,32,8192]{2,1,0:T(8,128)}) fusion(f32[1,32,8192]{2,1,0:T(8,128)S(1)} %copy-done.3, f32[32,8192]{1,0:T(8,128)S(1)} %copy-done.1, f32[32,8192]{1,0:T(8,128)} %reduce-scatter.2.cloned.1.call-done, f32[1,32,8192]{2,1,0:T(8,128)} %param.11, f32[1,32,8192]{2,1,0:T(8,128)} %param.12), kind=kLoop, calls=%fused_computation.4 | loop fusion | flops 4194304 | bytes 8388608 | tf_op jit(solution)/shard_map/sub | solution.py:47
  113.6 0.0 all-reduce.2.cloned.1.call-update
  113.7 51.0 %all-reduce.2.cloned.1.call-done = f32[32,8192]{1,0:T(8,128)} async-done(((f32[32,8192]{1,0:T(8,128)}), f32[32,8192]{1,0:T(8,128)}) %all-reduce.2.cloned.1.call-update) | async-done | bytes 1048592 | tf_op jit(solution)/shard_map/psum | solution.py:50
  164.7 2.1 %multiply_reduce_fusion = f32[]{:T(128)} fusion(f32[32,8192]{1,0:T(8,128)} %all-reduce.2.cloned.1.call-done), kind=kLoop, calls=%fused_computation.11 | loop fusion | flops 786431 | bytes 1048580 | tf_op jit(solution)/shard_map/reduce_sum | solution.py:51
  166.8 17.0 %psum.15 = f32[]{:T(128)} all-reduce(f32[]{:T(128)} %multiply_reduce_fusion), channel_id=1, replica_groups=mesh['rep'=4,'fsdp'=8] {'fsdp'}, use_global_device_ids=true, to_apply=%region_3.0 | all-reduce | flops 1 | bytes 8 | tf_op jit(solution)/shard_map/psum | solution.py:51
  184.5 0.0 copy-done.2
  184.5 2.8 %multiply_subtract_fusion = (f32[32,8192]{1,0:T(8,128)}, f32[32,8192]{1,0:T(8,128)}) fusion(f32[32,8192]{1,0:T(8,128)S(1)} %copy-done.1, f32[32,8192]{1,0:T(8,128)} %all-reduce.2.cloned.1.call-done, f32[]{:T(128)S(6)} %mul.75, f32[32,8192]{1,0:T(8,128)S(1)} %copy-done.2), kind=kLoop, calls=%fused_computation.10 | loop fusion | flops 1835008 | bytes 5242884 | tf_op jit(solution)/shard_map/sub | solution.py:23
Async XLA Ops:
  7.2 1.0 copy-start
  7.2 102.4 %reduce-scatter.2.cloned.1.call-start = ((), (), s32[]{:S(2)}) async-start(), calls=%async_computation.1 | async-start | bytes 9437184 | tf_op jit(solution)/shard_map/reduce_scatter | solution.py:31
  17.1 92.5 %copy-start.1 = (f32[32,8192]{1,0:T(8,128)S(1)}, f32[32,8192]{1,0:T(8,128)}, u32[]{:S(2)}) copy-start(f32[32,8192]{1,0:T(8,128)} %param.9) | copy-start | bytes 3145732
  17.1 92.5 %copy-start.3 = (f32[1,32,8192]{2,1,0:T(8,128)S(1)}, f32[1,32,8192]{2,1,0:T(8,128)}, u32[]{:S(2)}) copy-start(f32[1,32,8192]{2,1,0:T(8,128)} %param.10) | copy-start | bytes 3145732
  17.1 167.4 %copy-start.2 = (f32[32,8192]{1,0:T(8,128)S(1)}, f32[32,8192]{1,0:T(8,128)}, u32[]{:S(2)}) copy-start(f32[32,8192]{1,0:T(8,128)} %param.13) | copy-start | bytes 3145732
  17.1 147.6 %all-reduce.2.cloned.1.call-start = ((), (), s32[]{:S(2)}) async-start(), calls=%async_computation.2 | async-start | bytes 2097152 | tf_op jit(solution)/shard_map/psum | solution.py:50
Sparse Core Ops, SparseCore 0:
  17.3 92.3 reduce-scatter.1
  113.8 50.8 all-reduce.1
where the time goes:
time: 194 us
  waiting for transfers between devices  144 us (74%)
  blocking collectives  17 us (9%)
  between operations  14.8 us (8%)
  matrix products  8.98 us (5%)
  other arithmetic  8.92 us (5%)
    reduce_scatter x1, waiting for transfers between devices, per_device(): lax.psum_scatter(lax.dot_general(activations, cotangent, (((0,), (0,)), (...  92.4 us
    psum x1, waiting for transfers between devices, per_device(): average = lax.psum(pseudo, 'rep') / replicas  51 us
    psum x1, blocking collectives, per_device(): squares = lax.psum(jnp.sum(average * average), 'fsdp')  17 us
    dot_general x1, matrix products, per_device(): lax.dot_general(activations, cotangent, (((0,), (0,)), ((), ())), preferr...  8.98 us
    sub x1, other arithmetic, per_device(): pseudo = inner_rate * update - own_drift  4.03 us
  transfers between devices with their start and end apart: 2, of which 2 were waited for; matrix products, arithmetic and copies ran while one was open for 0% of the time, Pallas kernels for 0%

commit v1 on v0

v1 whole, which is shorter than its diff:
```python
import functools
import math

import jax
import jax.numpy as jnp
from jax import lax
from jax.experimental import pallas as pl
from jax.experimental.pallas import tpu as pltpu
from jax.sharding import PartitionSpec as P

INNER_STEP = 100
CORES = 2
CHUNKS = 16

beta_first = 0.9
beta_second = 0.95
inner_rate = 0.5
decay_weight = 0.1
outer_rate = 0.7
momentum_coef = 0.9
correction_one = 1.0 - beta_first**INNER_STEP
correction_two = 1.0 - beta_second**INNER_STEP

MESH = pl.DeviceIdType.MESH
ANCHOR, DRIFT, FIRST, SECOND, MOMENTUM = range(5)


def kernel(
    replicas, shards,
    acts_hbm, grads_hbm, anchor_hbm, drift_hbm, first_hbm, second_hbm, momentum_hbm,
    out_first, out_second, out_momentum, out_anchor,
    acts, acts_t, grads, part, swapped, chain, params, doubled, squares,
    acts_sem, grads_sem, params_sem, out_sem,
    swap_send, swap_recv, chain_send, chain_recv, double_send, double_recv,
    square_send, square_recv,
):
    chunks, _, width = grads.shape
    rows = params.shape[2]
    levels = shards // CORES
    stages = doubled.shape[0]
    rep = lax.axis_index("rep")
    shard = lax.axis_index("fsdp")
    z = shard // CORES
    core = shard % CORES
    other = 1 - core
    twin = (rep, z * CORES + other)
    above = (rep, lax.rem(shard + CORES, shards))
    below = (rep, lax.rem(shard + shards - CORES, shards))
    partners = []
    for stage in range(stages):
        bit = 2**stage
        partners.append(rep + bit - 2 * bit * ((rep // bit) % 2))

    barrier = pltpu.get_barrier_semaphore()

    @pl.loop(1, shards)
    def _(step):
        pl.semaphore_signal(
            barrier, inc=1, device_id=(rep, lax.rem(shard + step, shards)), device_id_type=MESH
        )

    for partner in partners:
        pl.semaphore_signal(barrier, inc=1, device_id=(partner, shard), device_id_type=MESH)

    def columns(k):
        return pl.ds(pl.multiple_of(k * width, width), width)

    def load_acts():
        return pltpu.make_async_copy(acts_hbm.at[0], acts, acts_sem)

    def load_grads(k):
        return pltpu.make_async_copy(
            grads_hbm.at[0, :, columns(k)], grads.at[k], grads_sem.at[k]
        )

    def load_param(which, k):
        source = (
            anchor_hbm, drift_hbm.at[0], first_hbm.at[0], second_hbm.at[0], momentum_hbm
        )[which]
        return pltpu.make_async_copy(
            source.at[:, columns(k)], params.at[which, k], params_sem.at[which, k]
        )

    def store_out(which, k):
        target = {
            FIRST: out_first.at[0], SECOND: out_second.at[0],
            MOMENTUM: out_momentum, ANCHOR: out_anchor,
        }[which]
        return pltpu.make_async_copy(
            params.at[which, k], target.at[:, columns(k)], out_sem.at[which, k]
        )

    load_acts().start()

    @pl.loop(0, chunks)
    def _(k):
        load_grads(k).start()

    @pl.loop(0, chunks)
    def _(k):
        for which in range(5):
            load_param(which, k).start()

    load_acts().wait()
    acts_t[...] = acts[...].T
    squares[shard] = jnp.zeros((8, 128), jnp.float32)
    pl.semaphore_wait(barrier, shards - 1 + stages)

    def swap(k):
        return pltpu.make_async_remote_copy(
            src_ref=part.at[k, other], dst_ref=swapped.at[k],
            send_sem=swap_send.at[k], recv_sem=swap_recv.at[k],
            device_id=twin, device_id_type=MESH,
        )

    def hop(k, dest, slot, target):
        return pltpu.make_async_remote_copy(
            src_ref=part.at[k, core, dest], dst_ref=chain.at[k, slot],
            send_sem=chain_send.at[k, dest], recv_sem=chain_recv.at[k, slot],
            device_id=target, device_id_type=MESH,
        )

    def double(stage, k):
        turn = lax.rem(k + stage, stages)
        partner = partners[0]
        for j in range(1, stages):
            partner = jnp.where(turn == j, partners[j], partner)
        source = params.at[DRIFT, k] if stage == 0 else doubled.at[stage - 1, k]
        return pltpu.make_async_remote_copy(
            src_ref=source, dst_ref=doubled.at[stage, k],
            send_sem=double_send.at[stage, k], recv_sem=double_recv.at[stage, k],
            device_id=(partner, shard), device_id_type=MESH,
        )

    def inside(k):
        return (k >= 0) & (k < chunks)

    def product(k):
        load_grads(k).wait()
        for at in range(0, width, 256):
            block = jnp.dot(
                acts_t[...], grads[k, :, at : at + 256], preferred_element_type=jnp.float32
            )
            for j in range(shards):
                part[k, j % CORES, j // CORES, :, at : at + 256] = block[j * rows : (j + 1) * rows]
        swap(k).start()

    def join(k):
        swap(k).wait_recv()
        part[k, core] += swapped[k]

    def add_hop(k, dest):
        hop(k, dest, dest, above).wait_recv()
        part[k, core, dest] += chain[k, dest]

    def send_up(k):
        for dest in range(levels - 1, 0, -1):
            @pl.when(dest > z)
            def _():
                @pl.when(z > 0)
                def _():
                    add_hop(k, dest)

                hop(k, dest, dest, above).start()

    def send_down(k):
        for dest in range(levels - 1):
            @pl.when(dest < z)
            def _():
                @pl.when(z < levels - 1)
                def _():
                    add_hop(k, dest)

                hop(k, dest, jnp.where(dest == z - 1, levels, dest), below).start()

    def inner_step(k):
        @pl.when(z > 0)
        def _():
            hop(k, z, z, above).wait_recv()
            part[k, core, z] += chain[k, z]

        @pl.when(z < levels - 1)
        def _():
            hop(k, z, levels, above).wait_recv()
            part[k, core, z] += chain[k, levels]

        for which in range(4):
            load_param(which, k).wait()
        gradient = part[k, core, z]
        drift = params[DRIFT, k]
        moment_one = beta_first * params[FIRST, k] + (1.0 - beta_first) * gradient
        moment_two = beta_second * params[SECOND, k] + (1.0 - beta_second) * gradient * gradient
        update = moment_one / correction_one / (
            jnp.sqrt(moment_two / correction_two) + 1e-08
        ) + decay_weight * (params[ANCHOR, k] + drift)
        params[FIRST, k] = moment_one
        params[SECOND, k] = moment_two
        params[DRIFT, k] = inner_rate * update - drift
        double(0, k).start()
        store_out(FIRST, k).start()
        store_out(SECOND, k).start()

    def add_replica(stage, k):
        double(stage, k).wait_recv()
        mine = params[DRIFT, k] if stage == 0 else doubled[stage - 1, k]
        total = mine + doubled[stage, k]
        if stage < stages - 1:
            doubled[stage, k] = total
            double(stage + 1, k).start()
        else:
            average = total / replicas
            doubled[stage, k] = average
            square = average * average
            folded = jnp.zeros((8, 128), jnp.float32)
            for i in range(0, rows, 8):
                for j in range(0, width, 128):
                    folded += square[i : i + 8, j : j + 128]
            squares[shard] += folded

    depth = jnp.maximum(z, levels - 1 - z)

    @pl.loop(0, chunks + 1 + levels + stages)
    def _(tick):
        @pl.when(inside(tick))
        def _():
            product(tick)

        @pl.when(inside(tick - 1))
        def _():
            join(tick - 1)

        up = tick - 1 - z

        @pl.when(inside(up))
        def _():
            send_up(up)

        down = tick - 1 - (levels - 1 - z)

        @pl.when(inside(down))
        def _():
            send_down(down)

        for stage in range(stages - 1, -1, -1):
            now = tick - 2 - depth - stage

            @pl.when(inside(now))
            def _():
                add_replica(stage, now)

        own = tick - 1 - depth

        @pl.when(inside(own))
        def _():
            inner_step(own)

    def tell(owner, target):
        return pltpu.make_async_remote_copy(
            src_ref=squares.at[owner], dst_ref=squares.at[owner],
            send_sem=square_send.at[target], recv_sem=square_recv.at[owner],
            device_id=(rep, target), device_id_type=MESH,
        )

    @pl.loop(1, shards)
    def _(step):
        tell(shard, lax.rem(shard + step, shards)).start()

    @pl.loop(0, chunks)
    def _(k):
        swap(k).wait_send()
        for dest in range(levels):
            @pl.when(dest != z)
            def _():
                hop(k, dest, dest, above).wait_send()

        for stage in range(stages):
            double(stage, k).wait_send()
        load_param(MOMENTUM, k).wait()
        store_out(FIRST, k).wait()
        store_out(SECOND, k).wait()

    @pl.loop(1, shards)
    def _(step):
        tell(lax.rem(shard + step, shards), lax.rem(shard + step, shards)).wait_recv()

    total = squares[0]
    for owner in range(1, shards):
        total += squares[owner]
    norm = jnp.sqrt(jnp.sum(total, keepdims=True))
    ceiling = 0.3 * math.sqrt(rows * shards * chunks * width)
    factor = ceiling / jnp.maximum(norm, ceiling)

    @pl.loop(0, chunks)
    def _(k):
        scaled = factor * doubled[stages - 1, k]
        momentum = momentum_coef * params[MOMENTUM, k] + scaled
        params[MOMENTUM, k] = momentum
        params[ANCHOR, k] = params[ANCHOR, k] - outer_rate * (scaled + momentum_coef * momentum)
        store_out(MOMENTUM, k).start()
        store_out(ANCHOR, k).start()

    @pl.loop(0, chunks)
    def _(k):
        store_out(MOMENTUM, k).wait()
        store_out(ANCHOR, k).wait()

    @pl.loop(1, shards)
    def _(step):
        tell(shard, lax.rem(shard + step, shards)).wait_send()


def per_device(replicas, shards, *args):
    acts, grads, anchor = args[:3]
    tokens, features = acts.shape[1:]
    rows, width = anchor.shape[0], anchor.shape[1] // CHUNKS
    levels = shards // CORES
    stages = replicas.bit_length() - 1
    f32 = jnp.float32
    dma = pltpu.SemaphoreType.DMA
    scratch = [
        pltpu.VMEM((tokens, features), acts.dtype),
        pltpu.VMEM((features, tokens), acts.dtype),
        pltpu.VMEM((CHUNKS, tokens, width), grads.dtype),
        pltpu.VMEM((CHUNKS, CORES, levels, rows, width), f32),
        pltpu.VMEM((CHUNKS, levels, rows, width), f32),
        pltpu.VMEM((CHUNKS, levels + 1, rows, width), f32),
        pltpu.VMEM((5, CHUNKS, rows, width), f32),
        pltpu.VMEM((stages, CHUNKS, rows, width), f32),
        pltpu.VMEM((shards, 8, 128), f32),
        dma, dma((CHUNKS,)), dma((5, CHUNKS)), dma((5, CHUNKS)),
        dma((CHUNKS,)), dma((CHUNKS,)),
        dma((CHUNKS, levels)), dma((CHUNKS, levels + 1)),
        dma((stages, CHUNKS)), dma((stages, CHUNKS)),
        dma((shards,)), dma((shards,)),
    ]
    moment = jax.ShapeDtypeStruct((1,) + anchor.shape, f32)
    outer = jax.ShapeDtypeStruct(anchor.shape, f32)
    anywhere = pl.BlockSpec(memory_space=pl.ANY)
    return pl.pallas_call(
        functools.partial(kernel, replicas, shards),
        out_shape=(moment, moment, outer, outer),
        in_specs=[anywhere] * 7,
        out_specs=(anywhere,) * 4,
        scratch_shapes=scratch,
        compiler_params=pltpu.CompilerParams(
            collective_id=0, has_side_effects=True, vmem_limit_bytes=60 * 2**20
        ),
        cost_estimate=pl.CostEstimate(
            flops=2 * tokens * features * anchor.shape[1],
            bytes_accessed=2 * tokens * anchor.shape[1] + 9 * 4 * anchor.size,
            transcendentals=anchor.size,
        ),
        name="outer_step",
    )(*args)


def solution(mesh):
    shared = P("fsdp", None)
    own = P("rep", "fsdp", None)
    return jax.shard_map(
        functools.partial(per_device, mesh.shape["rep"], mesh.shape["fsdp"]),
        mesh=mesh,
        in_specs=(own, own, shared, own, own, own, shared),
        out_specs=(own, own, shared, shared),
        check_vma=False,
    )
```

time: 194 us -> 107 us (0.55)
  waiting for transfers between devices: 144 us -> 0 us
  Pallas kernels: 0 us -> 97.4 us
  blocking collectives: 17 us -> 0 us
  between operations: 14.8 us -> 0.64 us
  matrix products: 8.98 us -> 0 us
  other arithmetic: 8.92 us -> 0 us
  local copies, waits for them, and re-layouts: 0.91 us -> 9.05 us
    pallas_call x0 -> x1, Pallas kernels: none -> 97.4 us  [per_device(): pl.pallas_call(functools.partial(kernel, replicas, shards), out_shape=(mo...]
    reduce_scatter x1 -> x0, waiting for transfers between devices: 92.4 us -> none  [per_device(): lax.psum_scatter(lax.dot_general(activations, cotangent, (((0,), (0,)), (...]
    psum x1 -> x0, waiting for transfers between devices: 51 us -> none  [per_device(): average = lax.psum(pseudo, 'rep') / replicas]
    psum x1 -> x0, blocking collectives: 17 us -> none  [per_device(): squares = lax.psum(jnp.sum(average * average), 'fsdp')]
    dot_general x1 -> x0, matrix products: 8.98 us -> none  [per_device(): lax.dot_general(activations, cotangent, (((0,), (0,)), ((), ())), preferr...]
    unnamed x8 -> x4, local copies, waits for them, and re-layouts: 0.91 us -> 9.05 us
    sub x2 -> x0, other arithmetic: 6.82 us -> none  [the longest x1 4.03 us: per_device(): pseudo = inner_rate * update - own_drift]
    reduce_sum x1 -> x0, other arithmetic: 2.1 us -> none  [per_device(): squares = lax.psum(jnp.sum(average * average), 'fsdp')]
  transfers between devices with their start and end apart: 2 -> 0, of which waited for: 2 -> 0; matrix products, arithmetic and copies ran while one was open for 0% -> 0% of each run, Pallas kernels for 0% -> 0%
where the time goes in v1:
time: 107 us
  Pallas kernels  97.4 us (91%)
  local copies, waits for them, and re-layouts  9.05 us (8%)
    pallas_call x1, Pallas kernels, per_device(): pl.pallas_call(functools.partial(kernel, replicas, shards), out_shape=(mo...  97.4 us
    unnamed x4, local copies, waits for them, and re-layouts  9.05 us

profile of v1, /device:TPU:0, one launch (start us, length us, event | category | flops | bytes accessed | tf_op | source)
XLA Modules:
  0.0 107.1 jit_solution(6593817509790263573)
XLA Ops:
  0.6 97.4 %outer_step.1 = (f32[1,32,8192]{2,1,0:T(8,128)}, f32[1,32,8192]{2,1,0:T(8,128)}, f32[32,8192]{1,0:T(8,128)}, f32[32,8192]{1,0:T(8,128)}) custom-call(bf16[1,512,256]{2,1,0:T(8,128)(2,1)} %acts_hbm.1, bf16[1,512,8192]{2,1,0:T(8,128)(2,1)} %grads_hbm.1, f32[32,8192]{1,0:T(8,128)} %anchor_hbm.1, f32[1,32,8192]{2,1,0:T(8,128)} %drift_hbm.1, ...), custom_call_target="tpu_custom_call" | custom-call | flops 2147483648 | bytes 17825792 | tf_op jit(solution)/shard_map/outer_step/pallas_call | solution.py:339
  98.0 2.3 %copy.15 = f32[1,32,8192]{2,1,0:T(8,128)} copy(f32[1,32,8192]{2,1,0:T(8,128)} %get-tuple-element.8) | data formatting | bytes 2097152
  100.3 2.3 %copy.16 = f32[1,32,8192]{2,1,0:T(8,128)} copy(f32[1,32,8192]{2,1,0:T(8,128)} %get-tuple-element.9) | data formatting | bytes 2097152
  102.5 2.3 %copy.17 = f32[32,8192]{1,0:T(8,128)} copy(f32[32,8192]{1,0:T(8,128)} %get-tuple-element.10) | data formatting | bytes 2097152
  104.8 2.3 %copy.18 = f32[32,8192]{1,0:T(8,128)} copy(f32[32,8192]{1,0:T(8,128)} %get-tuple-element.11) | data formatting | bytes 2097152

commit v2 on v1

--- a/solution.py
+++ b/solution.py
@@ -23,19 +23,21 @@
 
 MESH = pl.DeviceIdType.MESH
 ANCHOR, DRIFT, FIRST, SECOND, MOMENTUM = range(5)
+AHEAD = 4
+SLACK = 2
 
 
 def kernel(
     replicas, shards,
     acts_hbm, grads_hbm, anchor_hbm, drift_hbm, first_hbm, second_hbm, momentum_hbm,
     out_first, out_second, out_momentum, out_anchor,
-    acts, acts_t, grads, part, swapped, chain, params, doubled, squares,
-    acts_sem, grads_sem, params_sem, out_sem,
+    acts, acts_t, grads, part, swapped, chain, pseudo, doubled, squares,
+    acts_sem, grads_sem, params_sem,
     swap_send, swap_recv, chain_send, chain_recv, double_send, double_recv,
     square_send, square_recv,
 ):
     chunks, _, width = grads.shape
-    rows = params.shape[2]
+    rows = pseudo.shape[1]
     levels = shards // CORES
     stages = doubled.shape[0]
     rep = lax.axis_index("rep")
@@ -74,32 +76,23 @@
         )
 
     def load_param(which, k):
-        source = (
-            anchor_hbm, drift_hbm.at[0], first_hbm.at[0], second_hbm.at[0], momentum_hbm
+        source, target = (
+            (anchor_hbm, out_anchor),
+            (drift_hbm.at[0], None),
+            (first_hbm.at[0], out_first.at[0]),
+            (second_hbm.at[0], out_second.at[0]),
+            (momentum_hbm, out_momentum),
         )[which]
         return pltpu.make_async_copy(
-            source.at[:, columns(k)], params.at[which, k], params_sem.at[which, k]
-        )
-
-    def store_out(which, k):
-        target = {
-            FIRST: out_first.at[0], SECOND: out_second.at[0],
-            MOMENTUM: out_momentum, ANCHOR: out_anchor,
-        }[which]
-        return pltpu.make_async_copy(
-            params.at[which, k], target.at[:, columns(k)], out_sem.at[which, k]
+            source.at[:, columns(k)],
+            pseudo.at[k] if which == DRIFT else target.at[:, columns(k)],
+            params_sem.at[which, k],
         )
 
     load_acts().start()
 
-    @pl.loop(0, chunks)
-    def _(k):
+    for k in range(AHEAD):
         load_grads(k).start()
-
-    @pl.loop(0, chunks)
-    def _(k):
-        for which in range(5):
-            load_param(which, k).start()
 
     load_acts().wait()
     acts_t[...] = acts[...].T
@@ -125,7 +118,7 @@
         partner = partners[0]
         for j in range(1, stages):
             partner = jnp.where(turn == j, partners[j], partner)
-        source = params.at[DRIFT, k] if stage == 0 else doubled.at[stage - 1, k]
+        source = pseudo.at[k] if stage == 0 else doubled.at[stage - 1, k]
         return pltpu.make_async_remote_copy(
             src_ref=source, dst_ref=doubled.at[stage, k],
             send_sem=double_send.at[stage, k], recv_sem=double_recv.at[stage, k],
@@ -137,6 +130,14 @@
 
     def product(k):
         load_grads(k).wait()
+
+        @pl.when(k + AHEAD < chunks)
+        def _():
+            load_grads(k + AHEAD).start()
+
+        for which in range(5):
+            load_param(which, k).start()
+
         for at in range(0, width, 256):
             block = jnp.dot(
                 acts_t[...], grads[k, :, at : at + 256], preferred_element_type=jnp.float32
@@ -186,23 +187,22 @@
 
         for which in range(4):
             load_param(which, k).wait()
+        here = columns(k)
         gradient = part[k, core, z]
-        drift = params[DRIFT, k]
-        moment_one = beta_first * params[FIRST, k] + (1.0 - beta_first) * gradient
-        moment_two = beta_second * params[SECOND, k] + (1.0 - beta_second) * gradient * gradient
+        drift = pseudo[k]
+        moment_one = beta_first * out_first[0, :, here] + (1.0 - beta_first) * gradient
+        moment_two = beta_second * out_second[0, :, here] + (1.0 - beta_second) * gradient * gradient
         update = moment_one / correction_one / (
             jnp.sqrt(moment_two / correction_two) + 1e-08
-        ) + decay_weight * (params[ANCHOR, k] + drift)
-        params[FIRST, k] = moment_one
-        params[SECOND, k] = moment_two
-        params[DRIFT, k] = inner_rate * update - drift
+        ) + decay_weight * (out_anchor[:, here] + drift)
+        pseudo[k] = inner_rate * update - drift
         double(0, k).start()
-        store_out(FIRST, k).start()
-        store_out(SECOND, k).start()
+        out_first[0, :, here] = moment_one
+        out_second[0, :, here] = moment_two
 
     def add_replica(stage, k):
         double(stage, k).wait_recv()
-        mine = params[DRIFT, k] if stage == 0 else doubled[stage - 1, k]
+        mine = pseudo[k] if stage == 0 else doubled[stage - 1, k]
         total = mine + doubled[stage, k]
         if stage < stages - 1:
             doubled[stage, k] = total
@@ -217,9 +217,9 @@
                     folded += square[i : i + 8, j : j + 128]
             squares[shard] += folded
 
-    depth = jnp.maximum(z, levels - 1 - z)
-
-    @pl.loop(0, chunks + 1 + levels + stages)
+    depth = SLACK * jnp.maximum(z, levels - 1 - z)
+
+    @pl.loop(0, chunks + 2 + SLACK * (levels - 1) + stages)
     def _(tick):
         @pl.when(inside(tick))
         def _():
@@ -229,13 +229,13 @@
         def _():
             join(tick - 1)
 
-        up = tick - 1 - z
+        up = tick - 1 - SLACK * z
 
         @pl.when(inside(up))
         def _():
             send_up(up)
 
-        down = tick - 1 - (levels - 1 - z)
+        down = tick - 1 - SLACK * (levels - 1 - z)
 
         @pl.when(inside(down))
         def _():
@@ -276,8 +276,6 @@
         for stage in range(stages):
             double(stage, k).wait_send()
         load_param(MOMENTUM, k).wait()
-        store_out(FIRST, k).wait()
-        store_out(SECOND, k).wait()
 
     @pl.loop(1, shards)
     def _(step):
@@ -292,21 +290,26 @@
 
     @pl.loop(0, chunks)
     def _(k):
+        here = columns(k)
         scaled = factor * doubled[stages - 1, k]
-        momentum = momentum_coef * params[MOMENTUM, k] + scaled
-        params[MOMENTUM, k] = momentum
-        params[ANCHOR, k] = params[ANCHOR, k] - outer_rate * (scaled + momentum_coef * momentum)
-        store_out(MOMENTUM, k).start()
-        store_out(ANCHOR, k).start()
-
-    @pl.loop(0, chunks)
-    def _(k):
-        store_out(MOMENTUM, k).wait()
-        store_out(ANCHOR, k).wait()
+        momentum = momentum_coef * out_momentum[:, here] + scaled
+        out_momentum[:, here] = momentum
+        out_anchor[:, here] -= outer_rate * (scaled + momentum_coef * momentum)
 
     @pl.loop(1, shards)
     def _(step):
         tell(shard, lax.rem(shard + step, shards)).wait_send()
+
+
+def store(*refs):
+    count = len(refs) // 2
+    copies = [
+        pltpu.make_async_copy(refs[i], refs[count + i], refs[-1].at[i]) for i in range(count)
+    ]
+    for copy in copies:
+        copy.start()
+    for copy in copies:
+        copy.wait()
 
 
 def per_device(replicas, shards, *args):
@@ -324,34 +327,44 @@
         pltpu.VMEM((CHUNKS, CORES, levels, rows, width), f32),
         pltpu.VMEM((CHUNKS, levels, rows, width), f32),
         pltpu.VMEM((CHUNKS, levels + 1, rows, width), f32),
-        pltpu.VMEM((5, CHUNKS, rows, width), f32),
+        pltpu.VMEM((CHUNKS, rows, width), f32),
         pltpu.VMEM((stages, CHUNKS, rows, width), f32),
         pltpu.VMEM((shards, 8, 128), f32),
-        dma, dma((CHUNKS,)), dma((5, CHUNKS)), dma((5, CHUNKS)),
+        dma, dma((CHUNKS,)), dma((5, CHUNKS)),
         dma((CHUNKS,)), dma((CHUNKS,)),
         dma((CHUNKS, levels)), dma((CHUNKS, levels + 1)),
         dma((stages, CHUNKS)), dma((stages, CHUNKS)),
         dma((shards,)), dma((shards,)),
     ]
-    moment = jax.ShapeDtypeStruct((1,) + anchor.shape, f32)
-    outer = jax.ShapeDtypeStruct(anchor.shape, f32)
+    shapes = ((1,) + anchor.shape,) * 2 + (anchor.shape,) * 2
     anywhere = pl.BlockSpec(memory_space=pl.ANY)
-    return pl.pallas_call(
+    results = pl.pallas_call(
         functools.partial(kernel, replicas, shards),
-        out_shape=(moment, moment, outer, outer),
-        in_specs=[anywhere] * 7,
-        out_specs=(anywhere,) * 4,
+        out_shape=tuple(pltpu.VMEM(shape, f32) for shape in shapes),
+        in_specs=[pl.BlockSpec(memory_space=pltpu.HBM)] * 7,
+        out_specs=(pl.BlockSpec(memory_space=pltpu.VMEM),) * 4,
         scratch_shapes=scratch,
         compiler_params=pltpu.CompilerParams(
-            collective_id=0, has_side_effects=True, vmem_limit_bytes=60 * 2**20
+            collective_id=0, has_side_effects=True, vmem_limit_bytes=56 * 2**20
         ),
         cost_estimate=pl.CostEstimate(
             flops=2 * tokens * features * anchor.shape[1],
-            bytes_accessed=2 * tokens * anchor.shape[1] + 9 * 4 * anchor.size,
+            bytes_accessed=2 * tokens * anchor.shape[1] + 5 * 4 * anchor.size,
             transcendentals=anchor.size,
         ),
         name="outer_step",
     )(*args)
+    return pl.pallas_call(
+        store,
+        out_shape=tuple(jax.ShapeDtypeStruct(shape, f32) for shape in shapes),
+        in_specs=[anywhere] * 4,
+        out_specs=(anywhere,) * 4,
+        scratch_shapes=[dma((4,))],
+        cost_estimate=pl.CostEstimate(
+            flops=0, bytes_accessed=4 * 4 * anchor.size, transcendentals=0
+        ),
+        name="store_results",
+    )(*results)
 
 
 def solution(mesh):

time: 107 us -> 231 us (2.16)
  Pallas kernels: 97.4 us -> 227 us
  local copies, waits for them, and re-layouts: 9.05 us -> 3.94 us
    pallas_call x1 -> x2, Pallas kernels: 97.4 us -> 227 us  [the longest x1 128 us: per_device(): pl.pallas_call(store, out_shape=tuple((jax.ShapeDtypeStruct(shape, f32) f...]
    unnamed x4 -> x8, local copies, waits for them, and re-layouts: 9.05 us -> 3.94 us
where the time goes in v2:
time: 231 us
  Pallas kernels  227 us (98%)
  local copies, waits for them, and re-layouts  3.94 us (2%)
    pallas_call x1, Pallas kernels, per_device(): pl.pallas_call(store, out_shape=tuple((jax.ShapeDtypeStruct(shape, f32) f...  128 us
    pallas_call x1, Pallas kernels, per_device(): pl.pallas_call(functools.partial(kernel, replicas, shards), out_shape=tup...  98.3 us

profile of v2, /device:TPU:0, one launch (start us, length us, event | category | flops | bytes accessed | tf_op | source)
XLA Modules:
  0.0 231.1 jit_solution(9139572952001060242)
XLA Ops:
  0.6 98.3 %outer_step.1 = (f32[1,32,8192]{2,1,0:T(8,128)S(1)}, f32[1,32,8192]{2,1,0:T(8,128)S(1)}, f32[32,8192]{1,0:T(8,128)S(1)}, f32[32,8192]{1,0:T(8,128)S(1)}) custom-call(bf16[1,512,256]{2,1,0:T(8,128)(2,1)} %acts_hbm.1, bf16[1,512,8192]{2,1,0:T(8,128)(2,1)} %grads_hbm.1, f32[32,8192]{1,0:T(8,128)} %anchor_hbm.1, f32[1,32,8192]{2,1,0:T(8,128)} %drift_hbm.1, ...), custom_call_target="tpu_custom_call" | custom-call | flops 2147483648 | bytes 13631488 | tf_op jit(solution)/shard_map/outer_step/pallas_call | solution.py:341
  99.0 0.0 copy-start
  99.0 1.0 copy-done
  99.9 0.0 copy-start.1
  99.9 1.0 copy-done.1
  100.9 0.0 copy-start.2
  101.0 1.0 copy-done.2
  101.9 0.0 copy-start.3
  101.9 1.0 copy-done.3
  102.9 128.2 %store_results.1 = (f32[1,32,8192]{2,1,0:T(8,128)}, f32[1,32,8192]{2,1,0:T(8,128)}, f32[32,8192]{1,0:T(8,128)}, f32[32,8192]{1,0:T(8,128)}) custom-call(f32[1,32,8192]{2,1,0:T(8,128)} %copy-done, f32[1,32,8192]{2,1,0:T(8,128)} %copy-done.1, f32[32,8192]{1,0:T(8,128)} %copy-done.2, f32[32,8192]{1,0:T(8,128)} %copy-done.3), custom_call_target="tpu_custom_call" | custom-call | bytes 4194304 | tf_op jit(solution)/shard_map/store_results/pallas_call | solution.py:357
Async XLA Ops:
  99.0 1.0 copy-start
  99.9 1.0 copy-start.1
  100.9 1.0 copy-start.2
  101.9 1.0 copy-start.3

commit v3 on v2

--- a/solution.py
+++ b/solution.py
@@ -10,7 +10,7 @@
 
 INNER_STEP = 100
 CORES = 2
-CHUNKS = 16
+CHUNKS = 8
 
 beta_first = 0.9
 beta_second = 0.95
@@ -23,7 +23,7 @@
 
 MESH = pl.DeviceIdType.MESH
 ANCHOR, DRIFT, FIRST, SECOND, MOMENTUM = range(5)
-AHEAD = 4
+AHEAD = 2
 SLACK = 2
 
 
@@ -219,7 +219,7 @@
 
     depth = SLACK * jnp.maximum(z, levels - 1 - z)
 
-    @pl.loop(0, chunks + 2 + SLACK * (levels - 1) + stages)
+    @pl.loop(0, chunks + 1 + SLACK * (levels - 1 + stages))
     def _(tick):
         @pl.when(inside(tick))
         def _():
@@ -242,7 +242,7 @@
             send_down(down)
 
         for stage in range(stages - 1, -1, -1):
-            now = tick - 2 - depth - stage
+            now = tick - 1 - depth - SLACK * (stage + 1)
 
             @pl.when(inside(now))
             def _():
@@ -357,7 +357,7 @@
     return pl.pallas_call(
         store,
         out_shape=tuple(jax.ShapeDtypeStruct(shape, f32) for shape in shapes),
-        in_specs=[anywhere] * 4,
+        in_specs=[pl.BlockSpec(memory_space=pltpu.VMEM)] * 4,
         out_specs=(anywhere,) * 4,
         scratch_shapes=[dma((4,))],
         cost_estimate=pl.CostEstimate(

time: 231 us -> 107 us (0.46)
  Pallas kernels: 227 us -> 102 us
    pallas_call x1, Pallas kernels: 128 us -> 4.21 us  [per_device(): pl.pallas_call(store, out_shape=tuple((jax.ShapeDtypeStruct(shape, f32) f...]
where the time goes in v3:
time: 107 us
  Pallas kernels  102 us (95%)
  local copies, waits for them, and re-layouts  3.94 us (4%)
    pallas_call x1, Pallas kernels, per_device(): pl.pallas_call(functools.partial(kernel, replicas, shards), out_shape=tup...  97.8 us
    pallas_call x1, Pallas kernels, per_device(): pl.pallas_call(store, out_shape=tuple((jax.ShapeDtypeStruct(shape, f32) f...  4.21 us
    unnamed x8, local copies, waits for them, and re-layouts  3.94 us

profile of v3, /device:TPU:0, one launch (start us, length us, event | category | flops | bytes accessed | tf_op | source)
XLA Modules:
  0.0 106.6 jit_solution(9619681129447427383)
XLA Ops:
  0.6 97.8 %outer_step.1 = (f32[1,32,8192]{2,1,0:T(8,128)S(1)}, f32[1,32,8192]{2,1,0:T(8,128)S(1)}, f32[32,8192]{1,0:T(8,128)S(1)}, f32[32,8192]{1,0:T(8,128)S(1)}) custom-call(bf16[1,512,256]{2,1,0:T(8,128)(2,1)} %acts_hbm.1, bf16[1,512,8192]{2,1,0:T(8,128)(2,1)} %grads_hbm.1, f32[32,8192]{1,0:T(8,128)} %anchor_hbm.1, f32[1,32,8192]{2,1,0:T(8,128)} %drift_hbm.1, ...), custom_call_target="tpu_custom_call" | custom-call | flops 2147483648 | bytes 13631488 | tf_op jit(solution)/shard_map/outer_step/pallas_call | solution.py:341
  98.4 0.0 copy-start
  98.4 1.0 copy-done
  99.4 0.0 copy-start.1
  99.4 1.0 copy-done.1
  100.4 0.0 copy-start.2
  100.4 1.0 copy-done.2
  101.4 0.0 copy-start.3
  101.4 1.0 copy-done.3
  102.3 4.2 %store_results.1 = (f32[1,32,8192]{2,1,0:T(8,128)}, f32[1,32,8192]{2,1,0:T(8,128)}, f32[32,8192]{1,0:T(8,128)}, f32[32,8192]{1,0:T(8,128)}) custom-call(f32[1,32,8192]{2,1,0:T(8,128)} %copy-done, f32[1,32,8192]{2,1,0:T(8,128)} %copy-done.1, f32[32,8192]{1,0:T(8,128)} %copy-done.2, f32[32,8192]{1,0:T(8,128)} %copy-done.3), custom_call_target="tpu_custom_call" | custom-call | bytes 4194304 | tf_op jit(solution)/shard_map/store_results/pallas_call | solution.py:357
Async XLA Ops:
  98.4 1.0 copy-start
  99.4 1.0 copy-start.1
  100.4 1.0 copy-start.2
  101.4 1.0 copy-start.3

commit v4 on v3

--- a/solution.py
+++ b/solution.py
@@ -10,7 +10,7 @@
 
 INNER_STEP = 100
 CORES = 2
-CHUNKS = 8
+CHUNKS = 16
 
 beta_first = 0.9
 beta_second = 0.95
@@ -23,7 +23,7 @@
 
 MESH = pl.DeviceIdType.MESH
 ANCHOR, DRIFT, FIRST, SECOND, MOMENTUM = range(5)
-AHEAD = 2
+AHEAD = 4
 SLACK = 2
 
 
@@ -48,6 +48,7 @@
     twin = (rep, z * CORES + other)
     above = (rep, lax.rem(shard + CORES, shards))
     below = (rep, lax.rem(shard + shards - CORES, shards))
+    opposite = (rep, (levels - 1 - z) * CORES + core)
     partners = []
     for stage in range(stages):
         bit = 2**stage
@@ -156,24 +157,36 @@
 
     def send_up(k):
         for dest in range(levels - 1, 0, -1):
-            @pl.when(dest > z)
+            first = 1 if dest == levels - 1 else 0
+
+            @pl.when((dest > z) & (z >= first))
             def _():
-                @pl.when(z > 0)
+                @pl.when(z > first)
                 def _():
                     add_hop(k, dest)
 
                 hop(k, dest, dest, above).start()
 
+        @pl.when(z == 0)
+        def _():
+            hop(k, levels - 1, levels + 1, opposite).start()
+
     def send_down(k):
         for dest in range(levels - 1):
-            @pl.when(dest < z)
+            first = levels - 2 if dest == 0 else levels - 1
+
+            @pl.when((dest < z) & (z <= first))
             def _():
-                @pl.when(z < levels - 1)
+                @pl.when(z < first)
                 def _():
                     add_hop(k, dest)
 
                 hop(k, dest, jnp.where(dest == z - 1, levels, dest), below).start()
 
+        @pl.when(z == levels - 1)
+        def _():
+            hop(k, 0, levels + 1, opposite).start()
+
     def inner_step(k):
         @pl.when(z > 0)
         def _():
@@ -184,6 +197,11 @@
         def _():
             hop(k, z, levels, above).wait_recv()
             part[k, core, z] += chain[k, levels]
+
+        @pl.when((z == 0) | (z == levels - 1))
+        def _():
+            hop(k, z, levels + 1, opposite).wait_recv()
+            part[k, core, z] += chain[k, levels + 1]
 
         for which in range(4):
             load_param(which, k).wait()
@@ -301,17 +319,6 @@
         tell(shard, lax.rem(shard + step, shards)).wait_send()
 
 
-def store(*refs):
-    count = len(refs) // 2
-    copies = [
-        pltpu.make_async_copy(refs[i], refs[count + i], refs[-1].at[i]) for i in range(count)
-    ]
-    for copy in copies:
-        copy.start()
-    for copy in copies:
-        copy.wait()
-
-
 def per_device(replicas, shards, *args):
     acts, grads, anchor = args[:3]
     tokens, features = acts.shape[1:]
@@ -326,19 +333,18 @@
         pltpu.VMEM((CHUNKS, tokens, width), grads.dtype),
         pltpu.VMEM((CHUNKS, CORES, levels, rows, width), f32),
         pltpu.VMEM((CHUNKS, levels, rows, width), f32),
-        pltpu.VMEM((CHUNKS, levels + 1, rows, width), f32),
+        pltpu.VMEM((CHUNKS, levels + 2, rows, width), f32),
         pltpu.VMEM((CHUNKS, rows, width), f32),
         pltpu.VMEM((stages, CHUNKS, rows, width), f32),
         pltpu.VMEM((shards, 8, 128), f32),
         dma, dma((CHUNKS,)), dma((5, CHUNKS)),
         dma((CHUNKS,)), dma((CHUNKS,)),
-        dma((CHUNKS, levels)), dma((CHUNKS, levels + 1)),
+        dma((CHUNKS, levels)), dma((CHUNKS, levels + 2)),
         dma((stages, CHUNKS)), dma((stages, CHUNKS)),
         dma((shards,)), dma((shards,)),
     ]
     shapes = ((1,) + anchor.shape,) * 2 + (anchor.shape,) * 2
-    anywhere = pl.BlockSpec(memory_space=pl.ANY)
-    results = pl.pallas_call(
+    return pl.pallas_call(
         functools.partial(kernel, replicas, shards),
         out_shape=tuple(pltpu.VMEM(shape, f32) for shape in shapes),
         in_specs=[pl.BlockSpec(memory_space=pltpu.HBM)] * 7,
@@ -354,18 +360,6 @@
         ),
         name="outer_step",
     )(*args)
-    return pl.pallas_call(
-        store,
-        out_shape=tuple(jax.ShapeDtypeStruct(shape, f32) for shape in shapes),
-        in_specs=[pl.BlockSpec(memory_space=pltpu.VMEM)] * 4,
-        out_specs=(anywhere,) * 4,
-        scratch_shapes=[dma((4,))],
-        cost_estimate=pl.CostEstimate(
-            flops=0, bytes_accessed=4 * 4 * anchor.size, transcendentals=0
-        ),
-        name="store_results",
-    )(*results)
-
 
 def solution(mesh):
     shared = P("fsdp", None)

time: 107 us -> 99.8 us (0.933)
  Pallas kernels: 102 us -> 95.1 us
    pallas_call x1 -> x0, Pallas kernels: 4.21 us -> none  [per_device(): pl.pallas_call(store, out_shape=tuple((jax.ShapeDtypeStruct(shape, f32) f...]
    pallas_call x1, Pallas kernels: 97.8 us -> 95.1 us  [per_device(): pl.pallas_call(functools.partial(kernel, replicas, shards), out_shape=tup...]
    unnamed x8 -> x4, local copies, waits for them, and re-layouts: 3.94 us -> 3.88 us
where the time goes in v4:
time: 99.8 us; the launch traced here: 99.7 us
  Pallas kernels  95.1 us (95%)
  local copies, waits for them, and re-layouts  3.88 us (4%)
    pallas_call x1, Pallas kernels, per_device(): pl.pallas_call(functools.partial(kernel, replicas, shards), out_shape=tup...  95.1 us
    unnamed x4, local copies, waits for them, and re-layouts  3.88 us

profile of v4, /device:TPU:0, one launch (start us, length us, event | category | flops | bytes accessed | tf_op | source)
XLA Modules:
  0.0 99.7 jit_solution(12653037480091051417)
XLA Ops:
  0.6 95.1 %outer_step.1 = (f32[1,32,8192]{2,1,0:T(8,128)S(1)}, f32[1,32,8192]{2,1,0:T(8,128)S(1)}, f32[32,8192]{1,0:T(8,128)S(1)}, f32[32,8192]{1,0:T(8,128)S(1)}) custom-call(bf16[1,512,256]{2,1,0:T(8,128)(2,1)} %acts_hbm.1, bf16[1,512,8192]{2,1,0:T(8,128)(2,1)} %grads_hbm.1, f32[32,8192]{1,0:T(8,128)} %anchor_hbm.1, f32[1,32,8192]{2,1,0:T(8,128)} %drift_hbm.1, ...), custom_call_target="tpu_custom_call" | custom-call | flops 2147483648 | bytes 13631488 | tf_op jit(solution)/shard_map/outer_step/pallas_call | solution.py:347
  95.8 1.0 copy.15
  96.7 1.0 copy.16
  97.7 1.0 copy.17
  98.7 1.0 copy.18

commit v5 on v4

--- a/solution.py
+++ b/solution.py
@@ -25,6 +25,7 @@
 ANCHOR, DRIFT, FIRST, SECOND, MOMENTUM = range(5)
 AHEAD = 4
 SLACK = 2
+HALVES = 2
 
 
 def kernel(
@@ -114,15 +115,14 @@
             device_id=target, device_id_type=MESH,
         )
 
-    def double(stage, k):
-        turn = lax.rem(k + stage, stages)
-        partner = partners[0]
-        for j in range(1, stages):
-            partner = jnp.where(turn == j, partners[j], partner)
-        source = pseudo.at[k] if stage == 0 else doubled.at[stage - 1, k]
+    def double(stage, k, half):
+        partner = partners[(stage + half) % stages]
+        size = rows // HALVES
+        some = pl.ds(half * size, size)
+        source = pseudo if stage == 0 else doubled.at[stage - 1]
         return pltpu.make_async_remote_copy(
-            src_ref=source, dst_ref=doubled.at[stage, k],
-            send_sem=double_send.at[stage, k], recv_sem=double_recv.at[stage, k],
+            src_ref=source.at[k, some], dst_ref=doubled.at[stage, k, some],
+            send_sem=double_send.at[stage, k, half], recv_sem=double_recv.at[stage, k, half],
             device_id=(partner, shard), device_id_type=MESH,
         )
 
@@ -214,17 +214,20 @@
             jnp.sqrt(moment_two / correction_two) + 1e-08
         ) + decay_weight * (out_anchor[:, here] + drift)
         pseudo[k] = inner_rate * update - drift
-        double(0, k).start()
+        for half in range(HALVES):
+            double(0, k, half).start()
         out_first[0, :, here] = moment_one
         out_second[0, :, here] = moment_two
 
     def add_replica(stage, k):
-        double(stage, k).wait_recv()
+        for half in range(HALVES):
+            double(stage, k, half).wait_recv()
         mine = pseudo[k] if stage == 0 else doubled[stage - 1, k]
         total = mine + doubled[stage, k]
         if stage < stages - 1:
             doubled[stage, k] = total
-            double(stage + 1, k).start()
+            for half in range(HALVES):
+                double(stage + 1, k, half).start()
         else:
             average = total / replicas
             doubled[stage, k] = average
@@ -235,6 +238,18 @@
                     folded += square[i : i + 8, j : j + 128]
             squares[shard] += folded
 
+    def settle(k):
+        swap(k).wait_send()
+        for dest in range(levels):
+            @pl.when(dest != z)
+            def _():
+                hop(k, dest, dest, above).wait_send()
+
+        for stage in range(stages):
+            for half in range(HALVES):
+                double(stage, k, half).wait_send()
+        load_param(MOMENTUM, k).wait()
+
     depth = SLACK * jnp.maximum(z, levels - 1 - z)
 
     @pl.loop(0, chunks + 1 + SLACK * (levels - 1 + stages))
@@ -265,6 +280,12 @@
             @pl.when(inside(now))
             def _():
                 add_replica(stage, now)
+
+        old = tick - 2 - depth - SLACK * stages
+
+        @pl.when((old >= 0) & (old < chunks - 1))
+        def _():
+            settle(old)
 
         own = tick - 1 - depth
 
@@ -283,17 +304,7 @@
     def _(step):
         tell(shard, lax.rem(shard + step, shards)).start()
 
-    @pl.loop(0, chunks)
-    def _(k):
-        swap(k).wait_send()
-        for dest in range(levels):
-            @pl.when(dest != z)
-            def _():
-                hop(k, dest, dest, above).wait_send()
-
-        for stage in range(stages):
-            double(stage, k).wait_send()
-        load_param(MOMENTUM, k).wait()
+    settle(chunks - 1)
 
     @pl.loop(1, shards)
     def _(step):
@@ -340,7 +351,7 @@
         dma, dma((CHUNKS,)), dma((5, CHUNKS)),
         dma((CHUNKS,)), dma((CHUNKS,)),
         dma((CHUNKS, levels)), dma((CHUNKS, levels + 2)),
-        dma((stages, CHUNKS)), dma((stages, CHUNKS)),
+        dma((stages, CHUNKS, HALVES)), dma((stages, CHUNKS, HALVES)),
         dma((shards,)), dma((shards,)),
     ]
     shapes = ((1,) + anchor.shape,) * 2 + (anchor.shape,) * 2

time: 99.8 us -> 99.5 us (level)
  no operation moved by 1% of the time
where the time goes in v5:
time: 99.5 us; the launch traced here: 99.4 us
  Pallas kernels  94.9 us (95%)
  local copies, waits for them, and re-layouts  3.88 us (4%)
    pallas_call x1, Pallas kernels, per_device(): pl.pallas_call(functools.partial(kernel, replicas, shards), out_shape=tup...  94.9 us
    unnamed x4, local copies, waits for them, and re-layouts  3.88 us

profile of v5, /device:TPU:0, one launch (start us, length us, event | category | flops | bytes accessed | tf_op | source)
XLA Modules:
  0.0 99.4 jit_solution(602809032349145846)
XLA Ops:
  0.6 94.9 %outer_step.1 = (f32[1,32,8192]{2,1,0:T(8,128)S(1)}, f32[1,32,8192]{2,1,0:T(8,128)S(1)}, f32[32,8192]{1,0:T(8,128)S(1)}, f32[32,8192]{1,0:T(8,128)S(1)}) custom-call(bf16[1,512,256]{2,1,0:T(8,128)(2,1)} %acts_hbm.1, bf16[1,512,8192]{2,1,0:T(8,128)(2,1)} %grads_hbm.1, f32[32,8192]{1,0:T(8,128)} %anchor_hbm.1, f32[1,32,8192]{2,1,0:T(8,128)} %drift_hbm.1, ...), custom_call_target="tpu_custom_call" | custom-call | flops 2147483648 | bytes 13631488 | tf_op jit(solution)/shard_map/outer_step/pallas_call | solution.py:358
  95.5 1.0 copy.15
  96.5 1.0 copy.16
  97.4 1.0 copy.17
  98.4 1.0 copy.18

commit v6 on v5

--- a/solution.py
+++ b/solution.py
@@ -10,7 +10,7 @@
 
 INNER_STEP = 100
 CORES = 2
-CHUNKS = 16
+CHUNKS = 8
 
 beta_first = 0.9
 beta_second = 0.95
@@ -23,7 +23,7 @@
 
 MESH = pl.DeviceIdType.MESH
 ANCHOR, DRIFT, FIRST, SECOND, MOMENTUM = range(5)
-AHEAD = 4
+AHEAD = 2
 SLACK = 2
 HALVES = 2
 

time: 99.5 us -> 102 us (1.025)
  Pallas kernels: 94.9 us -> 97.5 us
    pallas_call x1, Pallas kernels: 94.9 us -> 97.5 us  [per_device(): pl.pallas_call(functools.partial(kernel, replicas, shards), out_shape=tup...]
where the time goes in v6:
time: 102 us
  Pallas kernels  97.5 us (96%)
  local copies, waits for them, and re-layouts  3.88 us (4%)
    pallas_call x1, Pallas kernels, per_device(): pl.pallas_call(functools.partial(kernel, replicas, shards), out_shape=tup...  97.5 us
    unnamed x4, local copies, waits for them, and re-layouts  3.88 us

profile of v6, /device:TPU:0, one launch (start us, length us, event | category | flops | bytes accessed | tf_op | source)
XLA Modules:
  0.0 102.0 jit_solution(15427357441987249697)
XLA Ops:
  0.6 97.5 %outer_step.1 = (f32[1,32,8192]{2,1,0:T(8,128)S(1)}, f32[1,32,8192]{2,1,0:T(8,128)S(1)}, f32[32,8192]{1,0:T(8,128)S(1)}, f32[32,8192]{1,0:T(8,128)S(1)}) custom-call(bf16[1,512,256]{2,1,0:T(8,128)(2,1)} %acts_hbm.1, bf16[1,512,8192]{2,1,0:T(8,128)(2,1)} %grads_hbm.1, f32[32,8192]{1,0:T(8,128)} %anchor_hbm.1, f32[1,32,8192]{2,1,0:T(8,128)} %drift_hbm.1, ...), custom_call_target="tpu_custom_call" | custom-call | flops 2147483648 | bytes 13631488 | tf_op jit(solution)/shard_map/outer_step/pallas_call | solution.py:358
  98.1 1.0 copy.15
  99.1 1.0 copy.16
  100.1 1.0 copy.17
  101.0 1.0 copy.18

commit v7 on v6

--- a/solution.py
+++ b/solution.py
@@ -10,7 +10,7 @@
 
 INNER_STEP = 100
 CORES = 2
-CHUNKS = 8
+CHUNKS = 32
 
 beta_first = 0.9
 beta_second = 0.95
@@ -23,7 +23,7 @@
 
 MESH = pl.DeviceIdType.MESH
 ANCHOR, DRIFT, FIRST, SECOND, MOMENTUM = range(5)
-AHEAD = 2
+AHEAD = 8
 SLACK = 2
 HALVES = 2
 

time: 102 us -> 103 us (level)
  no operation moved by 1% of the time
where the time goes in v7:
time: 103 us
  Pallas kernels  98.3 us (95%)
  local copies, waits for them, and re-layouts  3.88 us (4%)
    pallas_call x1, Pallas kernels, per_device(): pl.pallas_call(functools.partial(kernel, replicas, shards), out_shape=tup...  98.3 us
    unnamed x4, local copies, waits for them, and re-layouts  3.88 us

profile of v7, /device:TPU:0, one launch (start us, length us, event | category | flops | bytes accessed | tf_op | source)
XLA Modules:
  0.0 102.8 jit_solution(9960365956191922832)
XLA Ops:
  0.6 98.3 %outer_step.1 = (f32[1,32,8192]{2,1,0:T(8,128)S(1)}, f32[1,32,8192]{2,1,0:T(8,128)S(1)}, f32[32,8192]{1,0:T(8,128)S(1)}, f32[32,8192]{1,0:T(8,128)S(1)}) custom-call(bf16[1,512,256]{2,1,0:T(8,128)(2,1)} %acts_hbm.1, bf16[1,512,8192]{2,1,0:T(8,128)(2,1)} %grads_hbm.1, f32[32,8192]{1,0:T(8,128)} %anchor_hbm.1, f32[1,32,8192]{2,1,0:T(8,128)} %drift_hbm.1, ...), custom_call_target="tpu_custom_call" | custom-call | flops 2147483648 | bytes 13631488 | tf_op jit(solution)/shard_map/outer_step/pallas_call | solution.py:358
  98.9 1.0 copy.15
  99.9 1.0 copy.16
  100.9 1.0 copy.17
  101.8 1.0 copy.18
